TPU v7x, 32 devices: a whole 2x2x4 slice. The times are simulated.
32 devices in a mesh: grp: 2 (over y), ka: 4 (over z), aux: 2 (over x), orb: 2 (over core).
Axes of the slice: x: 2, y: 2, z: 4, core: 2. Of those that a mesh axis runs over, the one named last changes fastest.
Arguments:
- chol_tiles: bfloat16 [4, 4, 1536, 384], P('grp', 'ka', 'aux', 'orb'), parts along dimension 0, may hold values from -6 to 6
- tile_exps: int32 [4, 4, 12], P('grp', 'ka', 'aux'), parts along dimension 0, may hold values from -2 to 2
- amplitudes: bfloat16 [4, 4, 4, 96, 96], P('grp', 'ka'), parts along dimension 0, may hold values from -0.3125 to 0.3125
- pair_table: int32 [4, 4], replicated, may hold values from 0 to 3, as said below
Outputs:
- dressed: bfloat16 [4, 4, 1536, 384], P('grp', 'ka', 'aux', 'orb'), parts along dimension 0
- cycle_block: float32 [4, 4, 96, 96], P('grp', 'ka', ('aux', 'orb')), parts along dimension 0
There are 2 independent parts, one for each index of `grp`. A program takes and returns all parts, laid end to end along the dimension named above; an argument that names none is the same for every part. Nothing has to cross between parts.
Inputs may be any that keep to these rules, and one draw needn't show every extreme that they name: pair_table[k, k2] is the label of the k-point whose momentum is that of k minus that of k2 on a closed lattice of 4 points; each row and column is a permutation.
All inputs are finite; a program needn't handle non-finite values.
Results may differ from a plain program's by a relative error of at most 0.008.
Values may be sent and summed in bfloat16 or wider, within the bound.
A program may use at most 64 MiB of HBM per device.

v0:
```python
import jax
import jax.numpy as jnp
from jax import lax
from jax.sharding import PartitionSpec as P


def passed_along(shard, axis, by):
    devices = lax.axis_size(axis)
    return lax.ppermute(shard, axis, [(i, (i + by) % devices) for i in range(devices)])


def rescale(tile, exps):
    scale = jnp.repeat(jnp.exp2(exps.astype(jnp.float32)), 128, axis=-1)[..., None]
    return (tile.astype(jnp.float32) * scale).astype(jnp.bfloat16)


def body(chol_tiles, tile_exps, amplitudes, pair_table):
    nk = lax.axis_size("ka")
    mine = lax.axis_index("ka")
    nq, _, rows, vdev = chol_tiles.shape
    occ = amplitudes.shape[-1]
    qdev = rows // occ
    row_table = lax.dynamic_index_in_dim(pair_table, mine, 0, keepdims=False)
    own = rescale(chol_tiles, tile_exps)
    amp_rows = amplitudes[:, 0]

    def contribute(total, scaled, source):
        slot = row_table[source]
        amp = lax.dynamic_index_in_dim(amp_rows, slot, 1, keepdims=False)
        blocks = scaled[:, 0].reshape(nq, qdev, occ, vdev)
        return total + jnp.einsum("nij,nqja->nqia", amp, blocks, preferred_element_type=jnp.float32)

    payload = (chol_tiles, tile_exps)

    def unpack(item):
        return rescale(item[0], item[1])

    empty = jnp.zeros((nq, qdev, occ, vdev), jnp.float32)

    def advance(step, carry):
        parcel, total = carry
        total = contribute(total, unpack(parcel), (mine - step) % nk)
        parcel = passed_along((parcel[0], parcel[1]), "ka", 1)
        return (parcel, total)

    parcel, total = lax.fori_loop(0, nk - 1, advance, (payload, empty))
    total = contribute(total, unpack(parcel), (mine - (nk - 1)) % nk)
    dressed = total.astype(jnp.bfloat16)
    blocks = own[:, 0].reshape(nq, qdev, occ, vdev)
    norm = 1.0 / jnp.sqrt(jnp.float32(qdev * lax.axis_size("aux") * vdev * lax.axis_size("orb")))
    partial_cycle = (
        jnp.einsum("nqia,nqja->nij", dressed, blocks, preferred_element_type=jnp.float32) * norm
    )
    cycle = lax.psum_scatter(
        partial_cycle[:, None].astype(jnp.bfloat16), ("aux", "orb"), scatter_dimension=2, tiled=True
    ).astype(jnp.float32)
    return (dressed.reshape(nq, 1, rows, vdev), cycle)


def solution(mesh):
    return jax.shard_map(
        body,
        mesh=mesh,
        in_specs=(
            P("grp", "ka", "aux", "orb"),
            P("grp", "ka", "aux"),
            P("grp", "ka", None, None, None),
            P(),
        ),
        out_specs=(P("grp", "ka", "aux", "orb"), P("grp", "ka", ("aux", "orb"), None)),
        check_vma=False,
    )
```

profile of v0, /device:TPU:0, one launch (start us, length us, event | category | flops | bytes accessed | tf_op | source)
XLA Modules:
  0.0 102.8 jit_solution(7110625740767874442)
XLA Ops:
  7.9 1.3 %dynamic_slice.32 = s32[1,1]{1,0:T(1,128)} dynamic-slice(s32[4,4]{1,0:T(4,128)} %param.9, s32[]{:T(128)S(6)} %select_n.60, s32[]{:T(128)S(6)} %select_n.63), dynamic_slice_sizes={1,1} | dynamic-slice | bytes 12 | tf_op jit(solution)/shard_map/dynamic_slice | solution.py:28
  11.0 1.9 %copy.61 = bf16[2,1,768,192]{2,3,1,0:T(8,128)(2,1)} copy(bf16[2,1,768,192]{2,3,1,0:T(8,128)(2,1)} %param.6) | data formatting | bytes 1179648
  12.9 1.6 %copy.52 = bf16[2,1,4,96,96]{4,3,0,2,1:T(8,128)(2,1)} copy(bf16[2,1,4,96,96]{4,3,2,1,0:T(8,128)(2,1)} %param.8) | data formatting | bytes 294912 | tf_op args[2]
  14.5 53.7 %while.20 = (s32[]{:T(128)}, bf16[2,1,768,192]{2,3,1,0:T(8,128)(2,1)}, s32[2,1,6]{2,0,1:T(2,128)S(1)}, f32[2,8,96,192]{2,3,1,0:T(8,128)S(1)}, s32[]{:T(128)}, /*...) while((s32[]{:T(128)}, ...), condition=%wide.region_1.2_spmd.clone, body=%wide.region_0.1_spmd.clone.sunk | while | flops 58097708 | bytes 8921924 | solution.py:46
  14.5 1.1 %copy.65 = bf16[2,1,768,192]{2,3,1,0:T(8,128)(2,1)S(1)} copy(bf16[2,1,768,192]{2,3,1,0:T(8,128)(2,1)} %get-tuple-element.304) | data formatting | bytes 1179648 | tf_op jit(solution)/shard_map/while
  15.6 3.0 %collective-permute-start = (bf16[2,1,768,192]{2,3,1,0:T(8,128)(2,1)S(1)}, bf16[2,1,768,192]{2,3,1,0:T(8,128)(2,1)}, u32[]{:S(2)}, u32[]{:S(2)}) collective-permute-start(bf16[2,1,768,192]{2,3,1,0:T(8,128)(2,1)S(1)} %copy.65), channel_id=1, source_target_pairs={{0,4},{4,8},{8,12},{12,0},{1,5},{5,9},{9,13},{13,1},{2,6},{6,10},{... | collective-permute-start | bytes 1769480 | tf_op jit(solution)/shard_map/while/body/eval_jaxpr/ppermute | solution.py:9
  18.6 1.6 %collective-permute-start.1 = (s32[2,1,6]{2,0,1:T(2,128)S(1)}, s32[2,1,6]{2,0,1:T(2,128)S(1)}, u32[]{:S(2)}, u32[]{:S(2)}) collective-permute-start(s32[2,1,6]{2,0,1:T(2,128)S(1)} %copy.66), channel_id=1, source_target_pairs={{0,4},{4,8},{8,12},{12,0},{1,5},{5,9},{9,13},{13,1},{2,6},{6,10},{... | collective-permute-start | bytes 152 | tf_op jit(solution)/shard_map/while/body/eval_jaxpr/ppermute | solution.py:9
  22.3 0.8 squeeze.52
  23.8 1.5 %bitcast_add_fusion.3 = f32[2,8,96,192]{2,3,1,0:T(8,128)S(1)} fusion(f32[2,8,96,192]{2,3,1,0:T(8,128)S(1)} %get-tuple-element.306, bf16[2,8,96,192]{2,1,3,0:T(8,128)(2,1)S(1)} %squeeze.52, pred[]{:T(512)S(6)} %compare.5, bf16[2,4,96,96]{3,2,0,1:T(8,128)(2,1)} %get-tuple-element.320, s32[]{:T(128)S(6)} %select_n.73), kind=kOutput, calls=%fused_computation.clone.1 | convolution fusion | flops 57212928 | bytes 2998277 | tf_op jit(solution)/shard_map/while/body/eval_jaxpr/nij,nqja->nqia/dot_general | solution.py:31
  25.3 8.8 %collective-permute-done.1 = s32[2,1,6]{2,0,1:T(2,128)S(1)} collective-permute-done((s32[2,1,6]{2,0,1:T(2,128)S(1)}, s32[2,1,6]{2,0,1:T(2,128)S(1)}, u32[]{:S(2)}, u32[]{:S(2)}) %collective-permute-start.1) | collective-permute-done | bytes 80 | tf_op jit(solution)/shard_map/while/body/eval_jaxpr/ppermute | solution.py:9
  34.1 1.1 %copy.65 = bf16[2,1,768,192]{2,3,1,0:T(8,128)(2,1)S(1)} copy(bf16[2,1,768,192]{2,3,1,0:T(8,128)(2,1)} %get-tuple-element.304) | data formatting | bytes 1179648 | tf_op jit(solution)/shard_map/while
  35.2 1.3 %collective-permute-start.1 = (s32[2,1,6]{2,0,1:T(2,128)S(1)}, s32[2,1,6]{2,0,1:T(2,128)S(1)}, u32[]{:S(2)}, u32[]{:S(2)}) collective-permute-start(s32[2,1,6]{2,0,1:T(2,128)S(1)} %copy.66), channel_id=1, source_target_pairs={{0,4},{4,8},{8,12},{12,0},{1,5},{5,9},{9,13},{13,1},{2,6},{6,10},{... | collective-permute-start | bytes 152 | tf_op jit(solution)/shard_map/while/body/eval_jaxpr/ppermute | solution.py:9
  40.0 1.5 %bitcast_add_fusion.3 = f32[2,8,96,192]{2,3,1,0:T(8,128)S(1)} fusion(f32[2,8,96,192]{2,3,1,0:T(8,128)S(1)} %get-tuple-element.306, bf16[2,8,96,192]{2,1,3,0:T(8,128)(2,1)S(1)} %squeeze.52, pred[]{:T(512)S(6)} %compare.5, bf16[2,4,96,96]{3,2,0,1:T(8,128)(2,1)} %get-tuple-element.320, s32[]{:T(128)S(6)} %select_n.73), kind=kOutput, calls=%fused_computation.clone.1 | convolution fusion | flops 57212928 | bytes 2998277 | tf_op jit(solution)/shard_map/while/body/eval_jaxpr/nij,nqja->nqia/dot_general | solution.py:31
  41.6 10.0 %collective-permute-done.1 = s32[2,1,6]{2,0,1:T(2,128)S(1)} collective-permute-done((s32[2,1,6]{2,0,1:T(2,128)S(1)}, s32[2,1,6]{2,0,1:T(2,128)S(1)}, u32[]{:S(2)}, u32[]{:S(2)}) %collective-permute-start.1) | collective-permute-done | bytes 80 | tf_op jit(solution)/shard_map/while/body/eval_jaxpr/ppermute | solution.py:9
  51.6 1.1 %copy.65 = bf16[2,1,768,192]{2,3,1,0:T(8,128)(2,1)S(1)} copy(bf16[2,1,768,192]{2,3,1,0:T(8,128)(2,1)} %get-tuple-element.304) | data formatting | bytes 1179648 | tf_op jit(solution)/shard_map/while
  56.2 1.5 %bitcast_add_fusion.3 = f32[2,8,96,192]{2,3,1,0:T(8,128)S(1)} fusion(f32[2,8,96,192]{2,3,1,0:T(8,128)S(1)} %get-tuple-element.306, bf16[2,8,96,192]{2,1,3,0:T(8,128)(2,1)S(1)} %squeeze.52, pred[]{:T(512)S(6)} %compare.5, bf16[2,4,96,96]{3,2,0,1:T(8,128)(2,1)} %get-tuple-element.320, s32[]{:T(128)S(6)} %select_n.73), kind=kOutput, calls=%fused_computation.clone.1 | convolution fusion | flops 57212928 | bytes 2998277 | tf_op jit(solution)/shard_map/while/body/eval_jaxpr/nij,nqja->nqia/dot_general | solution.py:31
  57.8 10.4 %collective-permute-done.1 = s32[2,1,6]{2,0,1:T(2,128)S(1)} collective-permute-done((s32[2,1,6]{2,0,1:T(2,128)S(1)}, s32[2,1,6]{2,0,1:T(2,128)S(1)}, u32[]{:S(2)}, u32[]{:S(2)}) %collective-permute-start.1) | collective-permute-done | bytes 80 | tf_op jit(solution)/shard_map/while/body/eval_jaxpr/ppermute | solution.py:9
  68.3 1.2 %multiply_convert_fusion.2 = bf16[2,1,768,192]{2,3,1,0:T(8,128)(2,1)S(1)} fusion(bf16[2,1,768,192]{2,3,1,0:T(8,128)(2,1)} %get-tuple-element.182, f32[2,768]{1,0:T(2,128)S(1)} %bitcast.99), kind=kLoop, calls=%fused_computation.12 | loop fusion | flops 884736 | bytes 1185792 | tf_op jit(solution)/shard_map/convert_element_type | solution.py:14
  69.4 1.2 %copy.36 = bf16[2,1,768,192]{3,2,0,1:T(8,128)(2,1)} copy(bf16[2,1,768,192]{2,3,1,0:T(8,128)(2,1)S(1)} %multiply_convert_fusion.2) | data formatting | bytes 1179648 | tf_op jit(solution)/shard_map/reshape;squeeze | solution.py:30
  70.6 1.8 %copy.28 = f32[2,8,96,192]{3,2,1,0:T(8,128)} copy(f32[2,8,96,192]{2,3,1,0:T(8,128)S(1)} %get-tuple-element.181) | data formatting | bytes 2359296 | tf_op jit(solution)/shard_map/while | solution.py:46
  72.5 1.3 %multiply_convert_fusion.1 = bf16[2,1,768,192]{2,3,1,0:T(8,128)(2,1)S(1)} fusion(bf16[2,1,768,192]{2,3,1,0:T(8,128)(2,1)} %param.6, f32[2,768]{1,0:T(2,128)S(1)} %bitcast.100), kind=kLoop, calls=%fused_computation.11 | loop fusion | flops 884736 | bytes 1185792 | tf_op jit(solution)/shard_map/convert_element_type | solution.py:14
  74.6 1.5 %fusion.4 = bf16[2,8,96,192]{3,2,1,0:T(8,128)(2,1)S(1)} fusion(f32[2,8,96,192]{3,2,1,0:T(8,128)S(1)} %copy-done, bf16[2,8,96,192]{3,2,1,0:T(8,128)(2,1)} %bitcast.92, bf16[2,1,4,96,96]{4,3,2,1,0:T(8,128)(2,1)} %param.8, s32[]{:T(128)S(6)} %select_n.64), kind=kOutput, calls=%fused_computation.10 | convolution fusion | flops 57212928 | bytes 2605060 | tf_op jit(solution)/shard_map/nij,nqja->nqia/dot_general | solution.py:31
  77.3 1.1 %copy.31 = bf16[2,1,768,192]{2,3,1,0:T(8,128)(2,1)} copy(bf16[2,1,768,192]{3,2,0,1:T(8,128)(2,1)S(1)} %bitcast.90) | data formatting | bytes 1179648
  78.4 16.2 %reduce-scatter.4.cloned.1.call-done = bf16[24,192]{1,0:T(8,128)(2,1)} async-done(((bf16[96,192]{1,0:T(8,128)(2,1)}), bf16[24,192]{1,0:T(8,128)(2,1)}) %reduce-scatter.4.cloned.1.call-update) | async-done | bytes 9232
  (45 shorter events, 8.5 us)
Async XLA Ops:
  7.2 87.4 %reduce-scatter.4.cloned.1.call-start = ((), (), s32[]{:S(2)}) async-start(), calls=%async_computation.1 | async-start | bytes 61440
  15.6 18.5 %collective-permute-start = (bf16[2,1,768,192]{2,3,1,0:T(8,128)(2,1)S(1)}, bf16[2,1,768,192]{2,3,1,0:T(8,128)(2,1)}, u32[]{:S(2)}, u32[]{:S(2)}) collective-permute-start(bf16[2,1,768,192]{2,3,1,0:T(8,128)(2,1)S(1)} %copy.65), channel_id=1, source_target_pairs={{0,4},{4,8},{8,12},{12,0},{1,5},{5,9},{9,13},{13,1},{2,6},{6,10},{... | collective-permute-start | bytes 1769480 | tf_op jit(solution)/shard_map/while/body/eval_jaxpr/ppermute | solution.py:9
  18.6 15.5 %collective-permute-start.1 = (s32[2,1,6]{2,0,1:T(2,128)S(1)}, s32[2,1,6]{2,0,1:T(2,128)S(1)}, u32[]{:S(2)}, u32[]{:S(2)}) collective-permute-start(s32[2,1,6]{2,0,1:T(2,128)S(1)} %copy.66), channel_id=1, source_target_pairs={{0,4},{4,8},{8,12},{12,0},{1,5},{5,9},{9,13},{13,1},{2,6},{6,10},{... | collective-permute-start | bytes 152 | tf_op jit(solution)/shard_map/while/body/eval_jaxpr/ppermute | solution.py:9
  35.2 16.4 %collective-permute-start = (bf16[2,1,768,192]{2,3,1,0:T(8,128)(2,1)S(1)}, bf16[2,1,768,192]{2,3,1,0:T(8,128)(2,1)}, u32[]{:S(2)}, u32[]{:S(2)}) collective-permute-start(bf16[2,1,768,192]{2,3,1,0:T(8,128)(2,1)S(1)} %copy.65), channel_id=1, source_target_pairs={{0,4},{4,8},{8,12},{12,0},{1,5},{5,9},{9,13},{13,1},{2,6},{6,10},{... | collective-permute-start | bytes 1769480 | tf_op jit(solution)/shard_map/while/body/eval_jaxpr/ppermute | solution.py:9
  35.2 16.4 %collective-permute-start.1 = (s32[2,1,6]{2,0,1:T(2,128)S(1)}, s32[2,1,6]{2,0,1:T(2,128)S(1)}, u32[]{:S(2)}, u32[]{:S(2)}) collective-permute-start(s32[2,1,6]{2,0,1:T(2,128)S(1)} %copy.66), channel_id=1, source_target_pairs={{0,4},{4,8},{8,12},{12,0},{1,5},{5,9},{9,13},{13,1},{2,6},{6,10},{... | collective-permute-start | bytes 152 | tf_op jit(solution)/shard_map/while/body/eval_jaxpr/ppermute | solution.py:9
  52.7 15.5 %collective-permute-start = (bf16[2,1,768,192]{2,3,1,0:T(8,128)(2,1)S(1)}, bf16[2,1,768,192]{2,3,1,0:T(8,128)(2,1)}, u32[]{:S(2)}, u32[]{:S(2)}) collective-permute-start(bf16[2,1,768,192]{2,3,1,0:T(8,128)(2,1)S(1)} %copy.65), channel_id=1, source_target_pairs={{0,4},{4,8},{8,12},{12,0},{1,5},{5,9},{9,13},{13,1},{2,6},{6,10},{... | collective-permute-start | bytes 1769480 | tf_op jit(solution)/shard_map/while/body/eval_jaxpr/ppermute | solution.py:9
  52.7 15.5 %collective-permute-start.1 = (s32[2,1,6]{2,0,1:T(2,128)S(1)}, s32[2,1,6]{2,0,1:T(2,128)S(1)}, u32[]{:S(2)}, u32[]{:S(2)}) collective-permute-start(s32[2,1,6]{2,0,1:T(2,128)S(1)} %copy.66), channel_id=1, source_target_pairs={{0,4},{4,8},{8,12},{12,0},{1,5},{5,9},{9,13},{13,1},{2,6},{6,10},{... | collective-permute-start | bytes 152 | tf_op jit(solution)/shard_map/while/body/eval_jaxpr/ppermute | solution.py:9
  72.4 2.2 %copy-start = (f32[2,8,96,192]{3,2,1,0:T(8,128)S(1)}, f32[2,8,96,192]{3,2,1,0:T(8,128)}, u32[]{:S(2)}) copy-start(f32[2,8,96,192]{3,2,1,0:T(8,128)} %copy.28) | copy-start | bytes 3538948
Sparse Core Ops, SparseCore 0:
  77.4 17.0 reduce-scatter.3
where the time goes:
time: 104 us; the launch traced here: 103 us
  waiting for transfers between devices  45.4 us (44%)
  local copies, waits for them, and re-layouts  19.9 us (19%)
  between operations  15.8 us (15%)
  matrix products  6.49 us (6%)
  starting transfers between devices  5.94 us (6%)
  loops' own time  5.88 us (6%)
  other arithmetic  3.39 us (3%)
    ppermute x6, waiting for transfers between devices, passed_along(): lax.ppermute(shard, axis, [(i, (i + by) % devices) for i in range(devices)])  29.2 us
    unnamed x2, waiting for transfers between devices  16.2 us
    unnamed x13, local copies, waits for them, and re-layouts  6.99 us
    dot_general x4, matrix products, contribute(): jnp.einsum('nij,nqja->nqia', amp, blocks, preferred_element_type=jnp.floa...  6.11 us
    ppermute x6, starting transfers between devices, passed_along(): lax.ppermute(shard, axis, [(i, (i + by) % devices) for i in range(devices)])  5.9 us
    another operation x1, loops' own time, body(): parcel, total = lax.fori_loop(0, nk - 1, advance, (payload, empty))  5.88 us
    while x12, local copies, waits for them, and re-layouts  3.43 us
    dynamic_slice x4, local copies, waits for them, and re-layouts, contribute(): slot = row_table[source]  3.1 us
  transfers between devices with their start and end apart: 7, of which 4 were waited for; matrix products, arithmetic and copies ran while one was open for 10% of the time, Pallas kernels for 0%

commit v1 on v0

--- a/solution.py
+++ b/solution.py
@@ -1,7 +1,15 @@
+import functools
+
 import jax
 import jax.numpy as jnp
 from jax import lax
+from jax.experimental import pallas as pl
+from jax.experimental.pallas import tpu as pltpu
 from jax.sharding import PartitionSpec as P
+
+MESH = pl.DeviceIdType.MESH
+GROUP = 128
+LANES = 128
 
 
 def passed_along(shard, axis, by):
@@ -10,11 +18,11 @@
 
 
 def rescale(tile, exps):
-    scale = jnp.repeat(jnp.exp2(exps.astype(jnp.float32)), 128, axis=-1)[..., None]
+    scale = jnp.repeat(jnp.exp2(exps.astype(jnp.float32)), GROUP, axis=-1)[..., None]
     return (tile.astype(jnp.float32) * scale).astype(jnp.bfloat16)
 
 
-def body(chol_tiles, tile_exps, amplitudes, pair_table):
+def ring_body(chol_tiles, tile_exps, amplitudes, pair_table):
     nk = lax.axis_size("ka")
     mine = lax.axis_index("ka")
     nq, _, rows, vdev = chol_tiles.shape
@@ -30,21 +38,15 @@
         blocks = scaled[:, 0].reshape(nq, qdev, occ, vdev)
         return total + jnp.einsum("nij,nqja->nqia", amp, blocks, preferred_element_type=jnp.float32)
 
-    payload = (chol_tiles, tile_exps)
-
-    def unpack(item):
-        return rescale(item[0], item[1])
-
-    empty = jnp.zeros((nq, qdev, occ, vdev), jnp.float32)
-
     def advance(step, carry):
         parcel, total = carry
-        total = contribute(total, unpack(parcel), (mine - step) % nk)
-        parcel = passed_along((parcel[0], parcel[1]), "ka", 1)
+        total = contribute(total, rescale(*parcel), (mine - step) % nk)
+        parcel = passed_along(parcel, "ka", 1)
         return (parcel, total)
 
-    parcel, total = lax.fori_loop(0, nk - 1, advance, (payload, empty))
-    total = contribute(total, unpack(parcel), (mine - (nk - 1)) % nk)
+    empty = jnp.zeros((nq, qdev, occ, vdev), jnp.float32)
+    parcel, total = lax.fori_loop(0, nk - 1, advance, ((chol_tiles, tile_exps), empty))
+    total = contribute(total, rescale(*parcel), (mine - (nk - 1)) % nk)
     dressed = total.astype(jnp.bfloat16)
     blocks = own[:, 0].reshape(nq, qdev, occ, vdev)
     norm = 1.0 / jnp.sqrt(jnp.float32(qdev * lax.axis_size("aux") * vdev * lax.axis_size("orb")))
@@ -57,7 +59,267 @@
     return (dressed.reshape(nq, 1, rows, vdev), cycle)
 
 
+def line_kernel(
+    dims, chol, amps, scale, table, dressed, cycle,
+    tiles, own, rin, parts, asel, ain, wide, stage, pre, cyc, csend, crecv,
+    load_sem, store_sem, own_sem, fwd_sem, part_sem, in_sem, amp_sems, csend_sem, crecv_sem,
+):
+    nq, occ, vdev, pairs, norm = dims
+    pieces = nq * pairs
+    rem = vdev - LANES
+    step = 32
+    half = occ // step
+    me = lax.axis_index("ka")
+    aux = lax.axis_index("aux")
+    orb = lax.axis_index("orb")
+    is_end = jnp.logical_or(me == 0, me == 3)
+    is_mid = jnp.logical_not(is_end)
+    near = 1 + me // 3
+    outer = 3 * (me // 2)
+    across = 3 - me
+    peers = [(1 - aux, orb), (aux, 1 - orb), (1 - aux, 1 - orb)]
+
+    def load(p):
+        rows = pl.ds(pl.multiple_of((p % pairs) * 2 * occ, 2 * occ), 2 * occ)
+        return pltpu.make_async_copy(chol.at[p // pairs, 0, rows, :], tiles.at[p], load_sem.at[p])
+
+    def store(p):
+        rows = pl.ds(pl.multiple_of((p % pairs) * 2 * occ, 2 * occ), 2 * occ)
+        return pltpu.make_async_copy(stage.at[p], dressed.at[p // pairs, 0, rows, :], store_sem.at[p])
+
+    def send(src, slot, p, sem, to):
+        return pltpu.make_async_remote_copy(
+            src_ref=src.at[p], dst_ref=rin.at[slot, p], send_sem=sem.at[p], recv_sem=in_sem.at[slot, p],
+            device_id={"ka": to}, device_id_type=MESH,
+        )
+
+    def amp_send(to):
+        return pltpu.make_async_remote_copy(
+            src_ref=asel, dst_ref=ain, send_sem=amp_sems.at[0], recv_sem=amp_sems.at[1],
+            device_id={"ka": to}, device_id_type=MESH,
+        )
+
+    def loop(n, fn):
+        lax.fori_loop(0, n, lambda p, c: (fn(p), c)[1], 0)
+
+    loop(pieces, lambda p: load(p).start())
+
+    barrier = pltpu.get_barrier_semaphore()
+    for a, o in peers:
+        pl.semaphore_signal(barrier, inc=1, device_id={"aux": a, "orb": o}, device_id_type=MESH)
+
+    @pl.when(is_end)
+    def _():
+        pl.semaphore_signal(barrier, inc=1, device_id={"ka": near}, device_id_type=MESH)
+
+    @pl.when(is_mid)
+    def _():
+        pl.semaphore_signal(barrier, inc=1, device_id={"ka": outer}, device_id_type=MESH)
+        pl.semaphore_signal(barrier, inc=1, device_id={"ka": across}, device_id_type=MESH)
+
+    def amp(q, source):
+        return amps[q, 0, table[me, source]]
+
+    @pl.when(is_end)
+    def _():
+        for q in range(nq):
+            for slot, source in enumerate((near, 3 - near, 3 - me)):
+                asel[slot, q] = amp(q, source)
+
+    @pl.when(is_mid)
+    def _():
+        for q in range(nq):
+            for slot, source in enumerate((me, across, 3 - outer)):
+                wide[slot, q, pl.ds(0, occ), :] = amp(q, source)
+
+    def pack(p):
+        load(p).wait()
+        q, t = p // pairs, p % pairs
+        for i in range(half):
+            def rows(n):
+                s = scale[q, 0, (2 * half * t + n) * step // GROUP]
+                return tiles[p, pl.ds(n * step, step), :].astype(jnp.float32) * s
+            even, odd = rows(i), rows(i + half)
+            here = pl.ds(i * step, step)
+            own[p, here, pl.ds(0, LANES)] = even[:, :LANES].astype(jnp.bfloat16)
+            own[p, here, pl.ds(LANES, LANES)] = odd[:, :LANES].astype(jnp.bfloat16)
+            tail = jnp.concatenate([even[:, LANES:], odd[:, LANES:]], axis=1)
+            own[p, here, pl.ds(2 * LANES, 2 * rem)] = tail.astype(jnp.bfloat16)
+
+    def dot(a, b):
+        return jnp.dot(a, b, preferred_element_type=jnp.float32)
+
+    cyc[...] = jnp.zeros_like(cyc)
+
+    def finish(p, total):
+        q = p // pairs
+        y = total.astype(jnp.bfloat16)
+        cyc[q] += lax.dot_general(y, own[p], (((1,), (1,)), ((), ())), preferred_element_type=jnp.float32)
+        stage[p, pl.ds(0, occ), pl.ds(0, LANES)] = y[:, :LANES]
+        stage[p, pl.ds(occ, occ), pl.ds(0, LANES)] = y[:, LANES:2 * LANES]
+        stage[p, pl.ds(0, occ), pl.ds(LANES, rem)] = total[:, 2 * LANES:2 * LANES + rem].astype(jnp.bfloat16)
+        stage[p, pl.ds(occ, occ), pl.ds(LANES, rem)] = total[:, 2 * LANES + rem:].astype(jnp.bfloat16)
+        store(p).start()
+
+    pl.semaphore_wait(barrier, 4 + jnp.where(is_mid, 1, 0))
+
+    @pl.when(is_end)
+    def _():
+        amp_send(near).start()
+
+        def out(p):
+            pack(p)
+            send(own, 0, p, own_sem, near).start()
+
+        loop(pieces, out)
+
+        def first(p):
+            pre[p] = dot(amp(p // pairs, me), own[p])
+
+        loop(pieces, first)
+
+        def last(p):
+            send(own, 0, p, own_sem, near).wait_recv()
+            finish(p, pre[p] + rin[0, p].astype(jnp.float32))
+
+        loop(pieces, last)
+
+    @pl.when(is_mid)
+    def _():
+        def out(p):
+            pack(p)
+            send(own, 1, p, own_sem, across).start()
+
+        loop(pieces, out)
+        amp_send(outer).wait_recv()
+        for q in range(nq):
+            for slot in range(3):
+                wide[slot, q, pl.ds(occ, occ), :] = ain[slot, q]
+
+        def forward(p):
+            send(own, 0, p, own_sem, outer).wait_recv()
+            send(rin.at[0], 2, p, fwd_sem, across).start()
+
+        loop(pieces, forward)
+
+        def last(p):
+            q = p // pairs
+            both = dot(wide[0, q], own[p])
+            mine = dot(amp(q, outer), rin[0, p])
+            send(own, 1, p, own_sem, across).wait_recv()
+            both += dot(wide[1, q], rin[1, p])
+            send(own, 2, p, own_sem, across).wait_recv()
+            both += dot(wide[2, q], rin[2, p])
+            parts[p] = both[occ:].astype(jnp.bfloat16)
+            send(parts, 0, p, part_sem, outer).start()
+            finish(p, both[:occ] + mine)
+
+        loop(pieces, last)
+
+    part = occ // 4
+
+    def quarter(a, o):
+        rows = pl.ds(pl.multiple_of((2 * a + o) * part, 8), part)
+        return jnp.concatenate([cyc[q, rows, :] for q in range(nq)], axis=0)
+
+    def trade(n):
+        a, o = peers[n]
+        return pltpu.make_async_remote_copy(
+            src_ref=csend.at[n], dst_ref=crecv.at[n], send_sem=csend_sem.at[n], recv_sem=crecv_sem.at[n],
+            device_id={"aux": a, "orb": o}, device_id_type=MESH,
+        )
+
+    for n, (a, o) in enumerate(peers):
+        csend[n] = quarter(a, o).astype(jnp.bfloat16)
+        trade(n).start()
+    total = quarter(aux, orb)
+    for n in range(3):
+        trade(n).wait_recv()
+        total += crecv[n].astype(jnp.float32)
+    for q in range(nq):
+        cycle[q, 0] = total[q * part:(q + 1) * part] * norm
+
+    for n in range(3):
+        trade(n).wait_send()
+    loop(pieces, lambda p: store(p).wait())
+    loop(pieces, lambda p: send(own, 0, p, own_sem, near).wait_send())
+
+    @pl.when(is_end)
+    def _():
+        amp_send(near).wait_send()
+
+    @pl.when(is_mid)
+    def _():
+        loop(pieces, lambda p: send(own, 2, p, fwd_sem, across).wait_send())
+        loop(pieces, lambda p: send(own, 0, p, part_sem, outer).wait_send())
+
+
+def line_body(chol_tiles, tile_exps, amplitudes, pair_table):
+    nq, _, rows, vdev = chol_tiles.shape
+    occ = amplitudes.shape[-1]
+    pairs = rows // occ // 2
+    pieces = nq * pairs
+    width = 2 * vdev
+    devices = lax.axis_size("aux") * lax.axis_size("orb")
+    norm = (rows // occ * vdev * devices) ** -0.5
+    scale = jnp.exp2(tile_exps.astype(jnp.float32))
+    bf16, f32 = jnp.bfloat16, jnp.float32
+    dma = pltpu.SemaphoreType.DMA
+    part = occ // devices
+    return pl.pallas_call(
+        functools.partial(line_kernel, (nq, occ, vdev, pairs, norm)),
+        out_shape=(
+            jax.ShapeDtypeStruct(chol_tiles.shape, bf16),
+            jax.ShapeDtypeStruct((nq, 1, part, occ), f32),
+        ),
+        in_specs=[
+            pl.BlockSpec(memory_space=pl.ANY),
+            pl.BlockSpec(memory_space=pltpu.VMEM),
+            pl.BlockSpec(memory_space=pltpu.SMEM),
+            pl.BlockSpec(memory_space=pltpu.SMEM),
+        ],
+        out_specs=(pl.BlockSpec(memory_space=pl.ANY), pl.BlockSpec(memory_space=pltpu.VMEM)),
+        scratch_shapes=[
+            pltpu.VMEM((pieces, 2 * occ, vdev), bf16),
+            pltpu.VMEM((pieces, occ, width), bf16),
+            pltpu.VMEM((3, pieces, occ, width), bf16),
+            pltpu.VMEM((pieces, occ, width), bf16),
+            pltpu.VMEM((3, nq, occ, occ), bf16),
+            pltpu.VMEM((3, nq, occ, occ), bf16),
+            pltpu.VMEM((3, nq, 2 * occ, occ), bf16),
+            pltpu.VMEM((pieces, 2 * occ, vdev), bf16),
+            pltpu.VMEM((pieces, occ, width), f32),
+            pltpu.VMEM((nq, occ, occ), f32),
+            pltpu.VMEM((3, nq * part, occ), bf16),
+            pltpu.VMEM((3, nq * part, occ), bf16),
+            dma((pieces,)),
+            dma((pieces,)),
+            dma((pieces,)),
+            dma((pieces,)),
+            dma((pieces,)),
+            dma((3, pieces)),
+            dma((2,)),
+            dma((3,)),
+            dma((3,)),
+        ],
+        compiler_params=pltpu.CompilerParams(
+            collective_id=0, has_side_effects=True, vmem_limit_bytes=24 * 1024 * 1024
+        ),
+        cost_estimate=pl.CostEstimate(
+            flops=2 * 8 * occ * occ * width * pieces, bytes_accessed=4 * rows * nq * vdev, transcendentals=0
+        ),
+    )(chol_tiles, amplitudes, scale, pair_table)
+
+
 def solution(mesh):
+    def body(chol_tiles, tile_exps, amplitudes, pair_table):
+        nq, _, rows, vdev = chol_tiles.shape
+        occ = amplitudes.shape[-1]
+        line = mesh.shape["ka"] == 4 and mesh.shape["aux"] == 2 and mesh.shape["orb"] == 2
+        fits = rows % (2 * occ) == 0 and vdev == LANES + LANES // 2 and occ % 32 == 0
+        chosen = line_body if line and fits else ring_body
+        return chosen(chol_tiles, tile_exps, amplitudes, pair_table)
+
     return jax.shard_map(
         body,
         mesh=mesh,

time: 104 us -> 45.4 us (0.44)
  waiting for transfers between devices: 45.4 us -> 0 us
  Pallas kernels: 0 us -> 40.8 us
  local copies, waits for them, and re-layouts: 19.9 us -> 3.06 us
  between operations: 15.8 us -> 0.66 us
  matrix products: 6.49 us -> 0 us
  starting transfers between devices: 5.94 us -> 0 us
  loops' own time: 5.88 us -> 0 us
  other arithmetic: 3.39 us -> 0.69 us
    pallas_call x0 -> x1, Pallas kernels: none -> 40.8 us  [line_body(): pl.pallas_call(functools.partial(line_kernel, (nq, occ, vdev, pairs, norm...]
    ppermute x6 -> x0, waiting for transfers between devices: 29.2 us -> none  [passed_along(): lax.ppermute(shard, axis, [(i, (i + by) % devices) for i in range(devices)])]
    unnamed x2 -> x0, waiting for transfers between devices: 16.2 us -> none
    dot_general x5 -> x0, matrix products: 6.49 us -> none  [the longest x4 6.11 us: contribute(): jnp.einsum('nij,nqja->nqia', amp, blocks, preferred_element_type=jnp.floa...]
    ppermute x6 -> x0, starting transfers between devices: 5.9 us -> none  [passed_along(): lax.ppermute(shard, axis, [(i, (i + by) % devices) for i in range(devices)])]
    another operation x1 -> x0, loops' own time: 5.88 us -> none  [body(): parcel, total = lax.fori_loop(0, nk - 1, advance, (payload, empty))]
    while x13 -> x0, local copies, waits for them, and re-layouts: 5.19 us -> none
    unnamed x13 -> x6, local copies, waits for them, and re-layouts: 6.99 us -> 1.99 us
  transfers between devices with their start and end apart: 7 -> 0, of which waited for: 4 -> 0; matrix products, arithmetic and copies ran while one was open for 10% -> 0% of each run, Pallas kernels for 0% -> 0%
where the time goes in v1:
time: 45.4 us; the launch traced here: 45.2 us
  Pallas kernels  40.8 us (90%)
  local copies, waits for them, and re-layouts  3.06 us (7%)
  other arithmetic  0.69 us (2%)
  between operations  0.66 us (1%)
    pallas_call x1, Pallas kernels, line_body(): pl.pallas_call(functools.partial(line_kernel, (nq, occ, vdev, pairs, norm...  40.8 us
    unnamed x6, local copies, waits for them, and re-layouts  1.99 us
    pallas_call x1, local copies, waits for them, and re-layouts, line_body(): pl.pallas_call(functools.partial(line_kernel, (nq, occ, vdev, pairs, norm...  1.07 us

profile of v1, /device:TPU:0, one launch (start us, length us, event | category | flops | bytes accessed | tf_op | source)
XLA Modules:
  0.0 45.2 jit_solution(12198687837906913795)
XLA Ops:
  0.6 0.7 %multiply_exponential_fusion.scale = f32[2,1,6]{2,1,0:T(1,128)S(1)} fusion(s32[2,1,6]{2,1,0:T(1,128)} %param.5), kind=kLoop, calls=%fused_computation | loop fusion | flops 24 | bytes 96 | tf_op jit(solution)/shard_map/exp2 | solution.py:265
  1.3 0.0 copy-start
  1.3 0.0 copy-start.1
  1.3 1.4 %copy.6.chol = bf16[2,1,768,192]{3,2,1,0:T(8,128)(2,1)S(1)} copy(bf16[2,1,768,192]{2,3,1,0:T(8,128)(2,1)} %param.4) | data formatting | bytes 1179648 | tf_op args[0]
  2.7 0.0 copy-done
  2.7 0.0 copy-done.1
  2.7 40.8 %shard_map.59 = (bf16[2,1,768,192]{3,2,1,0:T(8,128)(2,1)S(1)}, f32[2,1,24,96]{3,2,1,0:T(8,128)S(1)}) custom-call(bf16[2,1,768,192]{3,2,1,0:T(8,128)(2,1)S(1)} %copy.6.chol, bf16[2,1,4,96,96]{4,3,2,1,0:T(8,128)(2,1)S(1)} %copy-done, f32[2,1,6]{2,1,0:T(1,128)S(1)} %multiply_exponential_fusion.scale, s32[4,4]{1,0:T(4,128)S(1)} %copy-done.1), custom_call_target="tpu_custom_call" | custom-call | flops 452984832 | bytes 1179648 | tf_op jit(solution)/shard_map/pallas_call | solution.py:269
  43.5 1.1 %copy.7 = bf16[2,1,768,192]{2,3,1,0:T(8,128)(2,1)} copy(bf16[2,1,768,192]{3,2,1,0:T(8,128)(2,1)S(1)} %get-tuple-element.2) | data formatting | bytes 1179648 | tf_op jit(solution)/shard_map/pallas_call | solution.py:269
  44.6 0.6 %copy.9 = f32[2,1,24,96]{3,2,1,0:T(8,128)} copy(f32[2,1,24,96]{3,2,1,0:T(8,128)S(1)} %get-tuple-element.7) | data formatting | bytes 36864
Async XLA Ops:
  1.3 1.4 %copy-start = (bf16[2,1,4,96,96]{4,3,2,1,0:T(8,128)(2,1)S(1)}, bf16[2,1,4,96,96]{4,3,2,1,0:T(8,128)(2,1)}, u32[]{:S(2)}) copy-start(bf16[2,1,4,96,96]{4,3,2,1,0:T(8,128)(2,1)} %amps.1) | copy-start | bytes 442372
  1.3 1.4 %copy-start.1 = (s32[4,4]{1,0:T(4,128)S(1)}, s32[4,4]{1,0:T(4,128)}, u32[]{:S(2)}) copy-start(s32[4,4]{1,0:T(4,128)} %table.1) | copy-start | bytes 196

commit v2 on v1

--- a/solution.py
+++ b/solution.py
@@ -1,4 +1,5 @@
 import functools
+import math
 
 import jax
 import jax.numpy as jnp
@@ -10,6 +11,8 @@
 MESH = pl.DeviceIdType.MESH
 GROUP = 128
 LANES = 128
+ROWS_EACH = 96
+LAG = 2
 
 
 def passed_along(shard, axis, by):
@@ -60,15 +63,14 @@
 
 
 def line_kernel(
-    dims, chol, amps, scale, table, dressed, cycle,
-    tiles, own, rin, parts, asel, ain, wide, stage, pre, cyc, csend, crecv,
+    dims, chol, amps, exps, table, dressed, cycle,
+    tiles, own, rin, parts, asel, ain, wide, mine, stage, pre, acc, cyc, csend, crecv,
     load_sem, store_sem, own_sem, fwd_sem, part_sem, in_sem, amp_sems, csend_sem, crecv_sem,
 ):
-    nq, occ, vdev, pairs, norm = dims
-    pieces = nq * pairs
-    rem = vdev - LANES
-    step = 32
-    half = occ // step
+    nq, occ, vdev, width, groups, rows_each, norm = dims
+    splits = vdev // rows_each
+    pieces = nq * groups * splits
+    blocks = width // occ
     me = lax.axis_index("ka")
     aux = lax.axis_index("aux")
     orb = lax.axis_index("orb")
@@ -79,13 +81,22 @@
     across = 3 - me
     peers = [(1 - aux, orb), (aux, 1 - orb), (1 - aux, 1 - orb)]
 
+    def q_of(p):
+        return p // (groups * splits)
+
+    def group_of(p):
+        return p // splits % groups
+
+    def window(ref, p):
+        high = pl.ds(pl.multiple_of(p % splits * rows_each, rows_each), rows_each)
+        lanes = pl.ds(pl.multiple_of(group_of(p) * width, width), width)
+        return ref.at[q_of(p), 0, high, lanes]
+
     def load(p):
-        rows = pl.ds(pl.multiple_of((p % pairs) * 2 * occ, 2 * occ), 2 * occ)
-        return pltpu.make_async_copy(chol.at[p // pairs, 0, rows, :], tiles.at[p], load_sem.at[p])
+        return pltpu.make_async_copy(window(chol, p), tiles.at[p], load_sem.at[p])
 
     def store(p):
-        rows = pl.ds(pl.multiple_of((p % pairs) * 2 * occ, 2 * occ), 2 * occ)
-        return pltpu.make_async_copy(stage.at[p], dressed.at[p // pairs, 0, rows, :], store_sem.at[p])
+        return pltpu.make_async_copy(stage.at[p], window(dressed, p), store_sem.at[p])
 
     def send(src, slot, p, sem, to):
         return pltpu.make_async_remote_copy(
@@ -126,55 +137,51 @@
             for slot, source in enumerate((near, 3 - near, 3 - me)):
                 asel[slot, q] = amp(q, source)
 
-    @pl.when(is_mid)
-    def _():
-        for q in range(nq):
-            for slot, source in enumerate((me, across, 3 - outer)):
-                wide[slot, q, pl.ds(0, occ), :] = amp(q, source)
-
     def pack(p):
         load(p).wait()
-        q, t = p // pairs, p % pairs
-        for i in range(half):
-            def rows(n):
-                s = scale[q, 0, (2 * half * t + n) * step // GROUP]
-                return tiles[p, pl.ds(n * step, step), :].astype(jnp.float32) * s
-            even, odd = rows(i), rows(i + half)
-            here = pl.ds(i * step, step)
-            own[p, here, pl.ds(0, LANES)] = even[:, :LANES].astype(jnp.bfloat16)
-            own[p, here, pl.ds(LANES, LANES)] = odd[:, :LANES].astype(jnp.bfloat16)
-            tail = jnp.concatenate([even[:, LANES:], odd[:, LANES:]], axis=1)
-            own[p, here, pl.ds(2 * LANES, 2 * rem)] = tail.astype(jnp.bfloat16)
-
-    def dot(a, b):
-        return jnp.dot(a, b, preferred_element_type=jnp.float32)
-
-    cyc[...] = jnp.zeros_like(cyc)
+        for n in range(width // LANES):
+            here = pl.ds(n * LANES, LANES)
+            shift = exps[q_of(p), 0, group_of(p) * (width // LANES) + n] + 8
+            s = lax.shift_left(1, shift).astype(jnp.float32) * (1.0 / 256.0)
+            own[p, :, here] = (tiles[p, :, here].astype(jnp.float32) * s).astype(jnp.bfloat16)
+
+    def spread(ref, at, block):
+        block = block.astype(jnp.float32)
+        for n in range(blocks):
+            strips = []
+            if n > 0:
+                strips.append(jnp.zeros((occ, n * occ), jnp.float32))
+            strips.append(block)
+            if n < blocks - 1:
+                strips.append(jnp.zeros((occ, (blocks - 1 - n) * occ), jnp.float32))
+            ref[(*at, pl.ds(n * occ, occ), slice(None))] = jnp.concatenate(strips, axis=1).astype(jnp.bfloat16)
+
+    def dot(x, w):
+        return lax.dot_general(x, w, (((1,), (1,)), ((), ())), preferred_element_type=jnp.float32)
 
     def finish(p, total):
-        q = p // pairs
         y = total.astype(jnp.bfloat16)
-        cyc[q] += lax.dot_general(y, own[p], (((1,), (1,)), ((), ())), preferred_element_type=jnp.float32)
-        stage[p, pl.ds(0, occ), pl.ds(0, LANES)] = y[:, :LANES]
-        stage[p, pl.ds(occ, occ), pl.ds(0, LANES)] = y[:, LANES:2 * LANES]
-        stage[p, pl.ds(0, occ), pl.ds(LANES, rem)] = total[:, 2 * LANES:2 * LANES + rem].astype(jnp.bfloat16)
-        stage[p, pl.ds(occ, occ), pl.ds(LANES, rem)] = total[:, 2 * LANES + rem:].astype(jnp.bfloat16)
+        stage[p] = y
         store(p).start()
+        acc[q_of(p)] += lax.dot_general(y, own[p], (((0,), (0,)), ((), ())), preferred_element_type=jnp.float32)
 
     pl.semaphore_wait(barrier, 4 + jnp.where(is_mid, 1, 0))
 
     @pl.when(is_end)
     def _():
-        amp_send(near).start()
-
         def out(p):
             pack(p)
             send(own, 0, p, own_sem, near).start()
 
-        loop(pieces, out)
+        out(0)
+        amp_send(near).start()
+        loop(pieces - 1, lambda p: out(p + 1))
+        acc[...] = jnp.zeros_like(acc)
+        for q in range(nq):
+            spread(mine, (q,), amp(q, me))
 
         def first(p):
-            pre[p] = dot(amp(p // pairs, me), own[p])
+            pre[p] = dot(own[p], mine[q_of(p)])
 
         loop(pieces, first)
 
@@ -187,36 +194,57 @@
     @pl.when(is_mid)
     def _():
         def out(p):
-            pack(p)
             send(own, 1, p, own_sem, across).start()
 
-        loop(pieces, out)
+        pack(0)
+        out(0)
+        pack(1)
+        out(1)
+        loop(pieces - 2, lambda p: pack(p + 2))
+        acc[...] = jnp.zeros_like(acc)
+        for q in range(nq):
+            spread(mine, (q,), amp(q, outer))
+            for slot, source in enumerate((me, across, 3 - outer)):
+                spread(wide, (slot, q, 0), amp(q, source))
         amp_send(outer).wait_recv()
         for q in range(nq):
             for slot in range(3):
-                wide[slot, q, pl.ds(occ, occ), :] = ain[slot, q]
+                spread(wide, (slot, q, 1), ain[slot, q])
 
         def forward(p):
             send(own, 0, p, own_sem, outer).wait_recv()
             send(rin.at[0], 2, p, fwd_sem, across).start()
 
-        loop(pieces, forward)
+            @pl.when(p + 2 < pieces)
+            def _():
+                out(p + 2)
 
         def last(p):
-            q = p // pairs
-            both = dot(wide[0, q], own[p])
-            mine = dot(amp(q, outer), rin[0, p])
+            q = q_of(p)
+            here = dot(own[p], wide[0, q, 0]) + dot(rin[0, p], mine[q])
+            there = dot(own[p], wide[0, q, 1])
             send(own, 1, p, own_sem, across).wait_recv()
-            both += dot(wide[1, q], rin[1, p])
+            there += dot(rin[1, p], wide[1, q, 1])
+            here += dot(rin[1, p], wide[1, q, 0])
             send(own, 2, p, own_sem, across).wait_recv()
-            both += dot(wide[2, q], rin[2, p])
-            parts[p] = both[occ:].astype(jnp.bfloat16)
+            parts[p] = (there + dot(rin[2, p], wide[2, q, 1])).astype(jnp.bfloat16)
             send(parts, 0, p, part_sem, outer).start()
-            finish(p, both[:occ] + mine)
-
-        loop(pieces, last)
+            finish(p, here + dot(rin[2, p], wide[2, q, 0]))
+
+        def turn(p):
+            @pl.when(p < pieces)
+            def _():
+                forward(p)
+
+            @pl.when(p >= LAG)
+            def _():
+                last(p - LAG)
+
+        loop(pieces + LAG, turn)
 
     part = occ // 4
+    for q in range(nq):
+        cyc[q] = sum(acc[q, n * occ:(n + 1) * occ, n * occ:(n + 1) * occ] for n in range(blocks))
 
     def quarter(a, o):
         rows = pl.ds(pl.multiple_of((2 * a + o) * part, 8), part)
@@ -257,38 +285,40 @@
 def line_body(chol_tiles, tile_exps, amplitudes, pair_table):
     nq, _, rows, vdev = chol_tiles.shape
     occ = amplitudes.shape[-1]
-    pairs = rows // occ // 2
-    pieces = nq * pairs
-    width = 2 * vdev
+    width = math.lcm(occ, LANES)
+    groups = rows // width
+    pieces = nq * groups * (vdev // ROWS_EACH)
     devices = lax.axis_size("aux") * lax.axis_size("orb")
     norm = (rows // occ * vdev * devices) ** -0.5
-    scale = jnp.exp2(tile_exps.astype(jnp.float32))
     bf16, f32 = jnp.bfloat16, jnp.float32
     dma = pltpu.SemaphoreType.DMA
     part = occ // devices
-    return pl.pallas_call(
-        functools.partial(line_kernel, (nq, occ, vdev, pairs, norm)),
+    turned = jnp.swapaxes(chol_tiles, 2, 3)
+    dressed, cycle = pl.pallas_call(
+        functools.partial(line_kernel, (nq, occ, vdev, width, groups, ROWS_EACH, norm)),
         out_shape=(
-            jax.ShapeDtypeStruct(chol_tiles.shape, bf16),
+            jax.ShapeDtypeStruct(turned.shape, bf16),
             jax.ShapeDtypeStruct((nq, 1, part, occ), f32),
         ),
         in_specs=[
-            pl.BlockSpec(memory_space=pl.ANY),
+            pl.BlockSpec(memory_space=pltpu.HBM),
             pl.BlockSpec(memory_space=pltpu.VMEM),
             pl.BlockSpec(memory_space=pltpu.SMEM),
             pl.BlockSpec(memory_space=pltpu.SMEM),
         ],
-        out_specs=(pl.BlockSpec(memory_space=pl.ANY), pl.BlockSpec(memory_space=pltpu.VMEM)),
+        out_specs=(pl.BlockSpec(memory_space=pltpu.HBM), pl.BlockSpec(memory_space=pltpu.VMEM)),
         scratch_shapes=[
-            pltpu.VMEM((pieces, 2 * occ, vdev), bf16),
-            pltpu.VMEM((pieces, occ, width), bf16),
-            pltpu.VMEM((3, pieces, occ, width), bf16),
-            pltpu.VMEM((pieces, occ, width), bf16),
+            pltpu.VMEM((pieces, ROWS_EACH, width), bf16),
+            pltpu.VMEM((pieces, ROWS_EACH, width), bf16),
+            pltpu.VMEM((3, pieces, ROWS_EACH, width), bf16),
+            pltpu.VMEM((pieces, ROWS_EACH, width), bf16),
             pltpu.VMEM((3, nq, occ, occ), bf16),
             pltpu.VMEM((3, nq, occ, occ), bf16),
-            pltpu.VMEM((3, nq, 2 * occ, occ), bf16),
-            pltpu.VMEM((pieces, 2 * occ, vdev), bf16),
-            pltpu.VMEM((pieces, occ, width), f32),
+            pltpu.VMEM((3, nq, 2, width, width), bf16),
+            pltpu.VMEM((nq, width, width), bf16),
+            pltpu.VMEM((pieces, ROWS_EACH, width), bf16),
+            pltpu.VMEM((pieces, ROWS_EACH, width), f32),
+            pltpu.VMEM((nq, width, width), f32),
             pltpu.VMEM((nq, occ, occ), f32),
             pltpu.VMEM((3, nq * part, occ), bf16),
             pltpu.VMEM((3, nq * part, occ), bf16),
@@ -306,9 +336,10 @@
             collective_id=0, has_side_effects=True, vmem_limit_bytes=24 * 1024 * 1024
         ),
         cost_estimate=pl.CostEstimate(
-            flops=2 * 8 * occ * occ * width * pieces, bytes_accessed=4 * rows * nq * vdev, transcendentals=0
+            flops=2 * 8 * occ * rows * vdev * nq, bytes_accessed=4 * rows * nq * vdev, transcendentals=0
         ),
-    )(chol_tiles, amplitudes, scale, pair_table)
+    )(turned, amplitudes, tile_exps, pair_table)
+    return jnp.swapaxes(dressed, 2, 3), cycle
 
 
 def solution(mesh):
@@ -316,7 +347,7 @@
         nq, _, rows, vdev = chol_tiles.shape
         occ = amplitudes.shape[-1]
         line = mesh.shape["ka"] == 4 and mesh.shape["aux"] == 2 and mesh.shape["orb"] == 2
-        fits = rows % (2 * occ) == 0 and vdev == LANES + LANES // 2 and occ % 32 == 0
+        fits = rows % math.lcm(occ, LANES) == 0 and vdev % ROWS_EACH == 0 and occ % 32 == 0
         chosen = line_body if line and fits else ring_body
         return chosen(chol_tiles, tile_exps, amplitudes, pair_table)
 

time: 45.4 us -> 49.5 us (1.090)
  Pallas kernels: 40.8 us -> 43.8 us
  local copies, waits for them, and re-layouts: 3.06 us -> 4.77 us
  other arithmetic: 0.69 us -> 0 us
    pallas_call x1, Pallas kernels: 40.8 us -> 43.8 us  [line_body(): pl.pallas_call(functools.partial(line_kernel, (nq, occ, vdev, width, grou...]
    unnamed x6 -> x10, local copies, waits for them, and re-layouts: 1.99 us -> 4.77 us
    pallas_call x1 -> x0, local copies, waits for them, and re-layouts: 1.07 us -> none  [line_body(): pl.pallas_call(functools.partial(line_kernel, (nq, occ, vdev, pairs, norm...]
    exp2 x1 -> x0, other arithmetic: 0.69 us -> none  [line_body(): scale = jnp.exp2(tile_exps.astype(jnp.float32))]
where the time goes in v2:
time: 49.5 us; the launch traced here: 49.3 us
  Pallas kernels  43.8 us (88%)
  local copies, waits for them, and re-layouts  4.77 us (10%)
  between operations  0.65 us (1%)
    pallas_call x1, Pallas kernels, line_body(): pl.pallas_call(functools.partial(line_kernel, (nq, occ, vdev, width, grou...  43.8 us
    unnamed x10, local copies, waits for them, and re-layouts  4.77 us

profile of v2, /device:TPU:0, one launch (start us, length us, event | category | flops | bytes accessed | tf_op | source)
XLA Modules:
  0.0 49.3 jit_solution(9839745771569663387)
XLA Ops:
  0.6 0.0 copy-start.3
  0.6 0.7 %copy-done.3 = s32[2,1,6]{2,1,0:T(1,128)S(1)} copy-done((s32[2,1,6]{2,1,0:T(1,128)S(1)}, s32[2,1,6]{2,1,0:T(1,128)}, u32[]{:S(2)}) %copy-start.3) | copy-done | bytes 72
  1.3 0.0 copy-start
  1.3 1.1 %copy-done = bf16[2,1,768,192]{2,3,1,0:T(8,128)(2,1)S(1)} copy-done((bf16[2,1,768,192]{2,3,1,0:T(8,128)(2,1)S(1)}, bf16[2,1,768,192]{2,3,1,0:T(8,128)(2,1)}, u32[]{:S(2)}) %copy-start) | copy-done | bytes 589848
  2.4 0.0 copy-start.1
  2.4 0.9 %copy-done.1 = bf16[2,1,4,96,96]{4,3,2,1,0:T(8,128)(2,1)S(1)} copy-done((bf16[2,1,4,96,96]{4,3,2,1,0:T(8,128)(2,1)S(1)}, bf16[2,1,4,96,96]{4,3,2,1,0:T(8,128)(2,1)}, u32[]{:S(2)}) %copy-start.1) | copy-done | bytes 147480
  3.3 0.0 copy-start.2
  3.3 0.7 %copy-done.2 = s32[4,4]{1,0:T(4,128)S(1)} copy-done((s32[4,4]{1,0:T(4,128)S(1)}, s32[4,4]{1,0:T(4,128)}, u32[]{:S(2)}) %copy-start.2) | copy-done | bytes 88
  4.0 43.8 %shard_map.59 = (bf16[2,1,192,768]{3,2,1,0:T(8,128)(2,1)S(1)}, f32[2,1,24,96]{3,2,1,0:T(8,128)S(1)}) custom-call(bf16[2,1,192,768]{3,2,1,0:T(8,128)(2,1)S(1)} %bitcast.3, bf16[2,1,4,96,96]{4,3,2,1,0:T(8,128)(2,1)S(1)} %copy-done.1, s32[2,1,6]{2,1,0:T(1,128)S(1)} %copy-done.3, s32[4,4]{1,0:T(4,128)S(1)} %copy-done.2), custom_call_target="tpu_custom_call" | custom-call | flops 452984832 | bytes 1179648 | tf_op jit(solution)/shard_map/pallas_call | solution.py:297
  47.8 0.8 %copy.8 = bf16[2,1,768,192]{2,3,1,0:T(8,128)(2,1)} copy(bf16[2,1,768,192]{2,3,1,0:T(8,128)(2,1)S(1)} %bitcast.2) | data formatting | bytes 1179648
  48.7 0.6 %copy.9 = f32[2,1,24,96]{3,2,1,0:T(8,128)} copy(f32[2,1,24,96]{3,2,1,0:T(8,128)S(1)} %get-tuple-element.9) | data formatting | bytes 36864
Async XLA Ops:
  0.6 0.7 %copy-start.3 = (s32[2,1,6]{2,1,0:T(1,128)S(1)}, s32[2,1,6]{2,1,0:T(1,128)}, u32[]{:S(2)}) copy-start(s32[2,1,6]{2,1,0:T(1,128)} %exps.1) | copy-start | bytes 148
  1.3 1.1 %copy-start = (bf16[2,1,768,192]{2,3,1,0:T(8,128)(2,1)S(1)}, bf16[2,1,768,192]{2,3,1,0:T(8,128)(2,1)}, u32[]{:S(2)}) copy-start(bf16[2,1,768,192]{2,3,1,0:T(8,128)(2,1)} %param.4) | copy-start | bytes 1769476
  2.4 0.9 %copy-start.1 = (bf16[2,1,4,96,96]{4,3,2,1,0:T(8,128)(2,1)S(1)}, bf16[2,1,4,96,96]{4,3,2,1,0:T(8,128)(2,1)}, u32[]{:S(2)}) copy-start(bf16[2,1,4,96,96]{4,3,2,1,0:T(8,128)(2,1)} %amps.1) | copy-start | bytes 442372
  3.3 0.7 %copy-start.2 = (s32[4,4]{1,0:T(4,128)S(1)}, s32[4,4]{1,0:T(4,128)}, u32[]{:S(2)}) copy-start(s32[4,4]{1,0:T(4,128)} %table.1) | copy-start | bytes 196

commit v3 on v2

--- a/solution.py
+++ b/solution.py
@@ -12,7 +12,7 @@
 GROUP = 128
 LANES = 128
 ROWS_EACH = 96
-LAG = 2
+BUNCH = 1
 
 
 def passed_along(shard, axis, by):
@@ -63,9 +63,9 @@
 
 
 def line_kernel(
-    dims, chol, amps, exps, table, dressed, cycle,
-    tiles, own, rin, parts, asel, ain, wide, mine, stage, pre, acc, cyc, csend, crecv,
-    load_sem, store_sem, own_sem, fwd_sem, part_sem, in_sem, amp_sems, csend_sem, crecv_sem,
+    dims, chol, amps_far, exps_far, table_far, dressed, cycle,
+    exps, table, tiles, amps, own, rin, parts, asel, ain, wide, mine, stage, pre, pre_there, acc, cyc, csend, crecv,
+    load_sem, store_sem, own_sem, fwd_sem, part_sem, in_sem, amp_sems, csend_sem, crecv_sem, amp_load_sem,
 ):
     nq, occ, vdev, width, groups, rows_each, norm = dims
     splits = vdev // rows_each
@@ -113,8 +113,6 @@
     def loop(n, fn):
         lax.fori_loop(0, n, lambda p, c: (fn(p), c)[1], 0)
 
-    loop(pieces, lambda p: load(p).start())
-
     barrier = pltpu.get_barrier_semaphore()
     for a, o in peers:
         pl.semaphore_signal(barrier, inc=1, device_id={"aux": a, "orb": o}, device_id_type=MESH)
@@ -128,8 +126,19 @@
         pl.semaphore_signal(barrier, inc=1, device_id={"ka": outer}, device_id_type=MESH)
         pl.semaphore_signal(barrier, inc=1, device_id={"ka": across}, device_id_type=MESH)
 
+    small = [
+        pltpu.make_async_copy(far, here, amp_load_sem.at[n])
+        for n, (far, here) in enumerate(((exps_far, exps), (table_far, table), (amps_far, amps)))
+    ]
+    for copy in small:
+        copy.start()
+    loop(pieces, lambda p: load(p).start())
+
     def amp(q, source):
         return amps[q, 0, table[me, source]]
+
+    for copy in small:
+        copy.wait()
 
     @pl.when(is_end)
     def _():
@@ -159,11 +168,41 @@
     def dot(x, w):
         return lax.dot_general(x, w, (((1,), (1,)), ((), ())), preferred_element_type=jnp.float32)
 
+    def bunch(ref, m):
+        return ref[pl.ds(m * BUNCH, BUNCH)].reshape(BUNCH * rows_each, width)
+
+    def put(ref, m, value):
+        ref[pl.ds(m * BUNCH, BUNCH)] = value.reshape(BUNCH, rows_each, width)
+
     def finish(p, total):
         y = total.astype(jnp.bfloat16)
         stage[p] = y
         store(p).start()
         acc[q_of(p)] += lax.dot_general(y, own[p], (((0,), (0,)), ((), ())), preferred_element_type=jnp.float32)
+
+    part = occ // 4
+
+    def quarter(q, a, o):
+        return cyc[q, pl.ds(pl.multiple_of((2 * a + o) * part, 8), part), :]
+
+    def trade(q, n):
+        a, o = peers[n]
+        return pltpu.make_async_remote_copy(
+            src_ref=csend.at[q, n], dst_ref=crecv.at[q, n], send_sem=csend_sem.at[q, n], recv_sem=crecv_sem.at[q, n],
+            device_id={"aux": a, "orb": o}, device_id_type=MESH,
+        )
+
+    def share(q):
+        cyc[q] = sum(acc[q, n * occ:(n + 1) * occ, n * occ:(n + 1) * occ] for n in range(blocks))
+        for n, (a, o) in enumerate(peers):
+            csend[q, n] = quarter(q, a, o)
+            trade(q, n).start()
+
+    def by_system(fn):
+        each = pieces // nq
+        for q in range(nq):
+            lax.fori_loop(q * each, (q + 1) * each, lambda p, c: (fn(p), c)[1], 0)
+            share(q)
 
     pl.semaphore_wait(barrier, 4 + jnp.where(is_mid, 1, 0))
 
@@ -180,27 +219,20 @@
         for q in range(nq):
             spread(mine, (q,), amp(q, me))
 
-        def first(p):
-            pre[p] = dot(own[p], mine[q_of(p)])
-
-        loop(pieces, first)
+        loop(pieces // BUNCH, lambda m: put(pre, m, dot(bunch(own, m), mine[q_of(m * BUNCH)])))
 
         def last(p):
             send(own, 0, p, own_sem, near).wait_recv()
             finish(p, pre[p] + rin[0, p].astype(jnp.float32))
 
-        loop(pieces, last)
+        by_system(last)
 
     @pl.when(is_mid)
     def _():
         def out(p):
             send(own, 1, p, own_sem, across).start()
 
-        pack(0)
-        out(0)
-        pack(1)
-        out(1)
-        loop(pieces - 2, lambda p: pack(p + 2))
+        loop(pieces, lambda p: (pack(p), out(p)))
         acc[...] = jnp.zeros_like(acc)
         for q in range(nq):
             spread(mine, (q,), amp(q, outer))
@@ -211,64 +243,42 @@
             for slot in range(3):
                 spread(wide, (slot, q, 1), ain[slot, q])
 
-        def forward(p):
-            send(own, 0, p, own_sem, outer).wait_recv()
-            send(rin.at[0], 2, p, fwd_sem, across).start()
-
-            @pl.when(p + 2 < pieces)
-            def _():
-                out(p + 2)
+        def early(m):
+            for n in range(BUNCH):
+                p = m * BUNCH + n
+                send(own, 0, p, own_sem, outer).wait_recv()
+                send(rin.at[0], 2, p, fwd_sem, across).start()
+            q = q_of(m * BUNCH)
+            x = bunch(own, m)
+            there = dot(x, wide[0, q, 1])
+            here = dot(x, wide[0, q, 0]) + dot(bunch(rin.at[0], m), mine[q])
+            for n in range(BUNCH):
+                send(own, 1, m * BUNCH + n, own_sem, across).wait_recv()
+            x = bunch(rin.at[1], m)
+            put(pre_there, m, there + dot(x, wide[1, q, 1]))
+            put(pre, m, here + dot(x, wide[1, q, 0]))
+
+        loop(pieces // BUNCH, early)
 
         def last(p):
             q = q_of(p)
-            here = dot(own[p], wide[0, q, 0]) + dot(rin[0, p], mine[q])
-            there = dot(own[p], wide[0, q, 1])
-            send(own, 1, p, own_sem, across).wait_recv()
-            there += dot(rin[1, p], wide[1, q, 1])
-            here += dot(rin[1, p], wide[1, q, 0])
             send(own, 2, p, own_sem, across).wait_recv()
-            parts[p] = (there + dot(rin[2, p], wide[2, q, 1])).astype(jnp.bfloat16)
+            parts[p] = (pre_there[p] + dot(rin[2, p], wide[2, q, 1])).astype(jnp.bfloat16)
             send(parts, 0, p, part_sem, outer).start()
-            finish(p, here + dot(rin[2, p], wide[2, q, 0]))
-
-        def turn(p):
-            @pl.when(p < pieces)
-            def _():
-                forward(p)
-
-            @pl.when(p >= LAG)
-            def _():
-                last(p - LAG)
-
-        loop(pieces + LAG, turn)
-
-    part = occ // 4
+            finish(p, pre[p] + dot(rin[2, p], wide[2, q, 0]))
+
+        by_system(last)
+
     for q in range(nq):
-        cyc[q] = sum(acc[q, n * occ:(n + 1) * occ, n * occ:(n + 1) * occ] for n in range(blocks))
-
-    def quarter(a, o):
-        rows = pl.ds(pl.multiple_of((2 * a + o) * part, 8), part)
-        return jnp.concatenate([cyc[q, rows, :] for q in range(nq)], axis=0)
-
-    def trade(n):
-        a, o = peers[n]
-        return pltpu.make_async_remote_copy(
-            src_ref=csend.at[n], dst_ref=crecv.at[n], send_sem=csend_sem.at[n], recv_sem=crecv_sem.at[n],
-            device_id={"aux": a, "orb": o}, device_id_type=MESH,
-        )
-
-    for n, (a, o) in enumerate(peers):
-        csend[n] = quarter(a, o).astype(jnp.bfloat16)
-        trade(n).start()
-    total = quarter(aux, orb)
-    for n in range(3):
-        trade(n).wait_recv()
-        total += crecv[n].astype(jnp.float32)
+        total = quarter(q, aux, orb)
+        for n in range(3):
+            trade(q, n).wait_recv()
+            total += crecv[q, n]
+        cycle[q, 0] = total * norm
+
     for q in range(nq):
-        cycle[q, 0] = total[q * part:(q + 1) * part] * norm
-
-    for n in range(3):
-        trade(n).wait_send()
+        for n in range(3):
+            trade(q, n).wait_send()
     loop(pieces, lambda p: store(p).wait())
     loop(pieces, lambda p: send(own, 0, p, own_sem, near).wait_send())
 
@@ -302,13 +312,16 @@
         ),
         in_specs=[
             pl.BlockSpec(memory_space=pltpu.HBM),
-            pl.BlockSpec(memory_space=pltpu.VMEM),
-            pl.BlockSpec(memory_space=pltpu.SMEM),
-            pl.BlockSpec(memory_space=pltpu.SMEM),
+            pl.BlockSpec(memory_space=pltpu.HBM),
+            pl.BlockSpec(memory_space=pltpu.HBM),
+            pl.BlockSpec(memory_space=pltpu.HBM),
         ],
         out_specs=(pl.BlockSpec(memory_space=pltpu.HBM), pl.BlockSpec(memory_space=pltpu.VMEM)),
         scratch_shapes=[
+            pltpu.SMEM(tile_exps.shape, jnp.int32),
+            pltpu.SMEM(pair_table.shape, jnp.int32),
             pltpu.VMEM((pieces, ROWS_EACH, width), bf16),
+            pltpu.VMEM(amplitudes.shape, bf16),
             pltpu.VMEM((pieces, ROWS_EACH, width), bf16),
             pltpu.VMEM((3, pieces, ROWS_EACH, width), bf16),
             pltpu.VMEM((pieces, ROWS_EACH, width), bf16),
@@ -318,10 +331,11 @@
             pltpu.VMEM((nq, width, width), bf16),
             pltpu.VMEM((pieces, ROWS_EACH, width), bf16),
             pltpu.VMEM((pieces, ROWS_EACH, width), f32),
+            pltpu.VMEM((pieces, ROWS_EACH, width), f32),
             pltpu.VMEM((nq, width, width), f32),
             pltpu.VMEM((nq, occ, occ), f32),
-            pltpu.VMEM((3, nq * part, occ), bf16),
-            pltpu.VMEM((3, nq * part, occ), bf16),
+            pltpu.VMEM((nq, 3, part, occ), f32),
+            pltpu.VMEM((nq, 3, part, occ), f32),
             dma((pieces,)),
             dma((pieces,)),
             dma((pieces,)),
@@ -329,16 +343,47 @@
             dma((pieces,)),
             dma((3, pieces)),
             dma((2,)),
-            dma((3,)),
+            dma((nq, 3)),
+            dma((nq, 3)),
             dma((3,)),
         ],
         compiler_params=pltpu.CompilerParams(
-            collective_id=0, has_side_effects=True, vmem_limit_bytes=24 * 1024 * 1024
+            collective_id=0, has_side_effects=True, vmem_limit_bytes=60 * 1024 * 1024
         ),
         cost_estimate=pl.CostEstimate(
             flops=2 * 8 * occ * rows * vdev * nq, bytes_accessed=4 * rows * nq * vdev, transcendentals=0
         ),
     )(turned, amplitudes, tile_exps, pair_table)
+
+    def hand_on(near_out, near_cycle, far_out, far_cycle, held, held_cycle, sems):
+        parts = [(q, 0, pl.ds(n * vdev // 2, vdev // 2)) for q in range(nq) for n in range(2)]
+        trips = [(near_cycle, held_cycle, far_cycle)] + [(near_out.at[i], held.at[i], far_out.at[i]) for i in parts]
+        ins = [pltpu.make_async_copy(a, b, sems.at[0, n]) for n, (a, b, _) in enumerate(trips)]
+        outs = [pltpu.make_async_copy(b, c, sems.at[1, n]) for n, (_, b, c) in enumerate(trips)]
+        for copy in ins:
+            copy.start()
+        for before, after in zip(ins, outs):
+            before.wait()
+            after.start()
+        for copy in outs:
+            copy.wait()
+
+    dressed, cycle = pl.pallas_call(
+        hand_on,
+        out_shape=(
+            jax.ShapeDtypeStruct(dressed.shape, dressed.dtype),
+            jax.ShapeDtypeStruct(cycle.shape, cycle.dtype),
+        ),
+        in_specs=[pl.BlockSpec(memory_space=pltpu.HBM)] * 2,
+        out_specs=(pl.BlockSpec(memory_space=pltpu.HBM),) * 2,
+        scratch_shapes=[
+            pltpu.VMEM(dressed.shape, dressed.dtype),
+            pltpu.VMEM(cycle.shape, cycle.dtype),
+            dma((2, 1 + 2 * nq)),
+        ],
+        compiler_params=pltpu.CompilerParams(vmem_limit_bytes=60 * 1024 * 1024),
+        name="hand_on",
+    )(dressed, cycle)
     return jnp.swapaxes(dressed, 2, 3), cycle
 
 
@@ -347,7 +392,7 @@
         nq, _, rows, vdev = chol_tiles.shape
         occ = amplitudes.shape[-1]
         line = mesh.shape["ka"] == 4 and mesh.shape["aux"] == 2 and mesh.shape["orb"] == 2
-        fits = rows % math.lcm(occ, LANES) == 0 and vdev % ROWS_EACH == 0 and occ % 32 == 0
+        fits = rows % math.lcm(occ, LANES) == 0 and vdev % (BUNCH * ROWS_EACH) == 0 and occ % 32 == 0
         chosen = line_body if line and fits else ring_body
         return chosen(chol_tiles, tile_exps, amplitudes, pair_table)
 

time: 49.5 us -> 42.6 us (0.86)
  local copies, waits for them, and re-layouts: 4.77 us -> 0 us
  Pallas kernels: 43.8 us -> 41.9 us
    unnamed x10 -> x0, local copies, waits for them, and re-layouts: 4.77 us -> none
    pallas_call x1, Pallas kernels: 43.8 us -> 40 us  [line_body(): pl.pallas_call(functools.partial(line_kernel, (nq, occ, vdev, width, grou...]
    pallas_call x0 -> x1, Pallas kernels: none -> 1.89 us  [line_body(): pl.pallas_call(hand_on, out_shape=(jax.ShapeDtypeStruct(dressed.shape, dr...]
where the time goes in v3:
time: 42.6 us; the launch traced here: 42.5 us
  Pallas kernels  41.9 us (98%)
  between operations  0.64 us (2%)
    pallas_call x1, Pallas kernels, line_body(): pl.pallas_call(functools.partial(line_kernel, (nq, occ, vdev, width, grou...  40 us
    pallas_call x1, Pallas kernels, line_body(): pl.pallas_call(hand_on, out_shape=(jax.ShapeDtypeStruct(dressed.shape, dr...  1.89 us

profile of v3, /device:TPU:0, one launch (start us, length us, event | category | flops | bytes accessed | tf_op | source)
XLA Modules:
  0.0 42.5 jit_solution(14868934923377163883)
XLA Ops:
  0.6 40.0 %shard_map.59 = (bf16[2,1,192,768]{3,2,1,0:T(8,128)(2,1)}, f32[2,1,24,96]{3,2,1,0:T(8,128)}) custom-call(bf16[2,1,192,768]{3,2,1,0:T(8,128)(2,1)} %bitcast.2, bf16[2,1,4,96,96]{4,3,2,1,0:T(8,128)(2,1)} %amps_far.1, s32[2,1,6]{2,1,0:T(1,128)} %exps_far.1, s32[4,4]{1,0:T(4,128)} %table_far.1), custom_call_target="tpu_custom_call" | custom-call | flops 452984832 | bytes 1179648 | tf_op jit(solution)/shard_map/pallas_call | solution.py:307
  40.6 1.9 %hand_on.1 = (bf16[2,1,192,768]{3,2,1,0:T(8,128)(2,1)}, f32[2,1,24,96]{3,2,1,0:T(8,128)}) custom-call(bf16[2,1,192,768]{3,2,1,0:T(8,128)(2,1)} %get-tuple-element.6.near_out, f32[2,1,24,96]{3,2,1,0:T(8,128)} %get-tuple-element.7.near_cycle), custom_call_target="tpu_custom_call" | custom-call | tf_op jit(solution)/shard_map/hand_on/pallas_call | solution.py:371

commit v4 on v3

--- a/solution.py
+++ b/solution.py
@@ -12,6 +12,8 @@
 GROUP = 128
 LANES = 128
 ROWS_EACH = 96
+AHEAD = 5
+LAG = 4
 BUNCH = 1
 
 
@@ -232,7 +234,8 @@
         def out(p):
             send(own, 1, p, own_sem, across).start()
 
-        loop(pieces, lambda p: (pack(p), out(p)))
+        loop(AHEAD, lambda p: (pack(p), out(p)))
+        loop(pieces - AHEAD, lambda p: pack(p + AHEAD))
         acc[...] = jnp.zeros_like(acc)
         for q in range(nq):
             spread(mine, (q,), amp(q, outer))
@@ -248,6 +251,11 @@
                 p = m * BUNCH + n
                 send(own, 0, p, own_sem, outer).wait_recv()
                 send(rin.at[0], 2, p, fwd_sem, across).start()
+
+                @pl.when(p + AHEAD < pieces)
+                def _():
+                    out(p + AHEAD)
+
             q = q_of(m * BUNCH)
             x = bunch(own, m)
             there = dot(x, wide[0, q, 1])
@@ -258,8 +266,6 @@
             put(pre_there, m, there + dot(x, wide[1, q, 1]))
             put(pre, m, here + dot(x, wide[1, q, 0]))
 
-        loop(pieces // BUNCH, early)
-
         def last(p):
             q = q_of(p)
             send(own, 2, p, own_sem, across).wait_recv()
@@ -267,7 +273,21 @@
             send(parts, 0, p, part_sem, outer).start()
             finish(p, pre[p] + dot(rin[2, p], wide[2, q, 0]))
 
-        by_system(last)
+        def turn(p):
+            @pl.when(p < pieces)
+            def _():
+                early(p)
+
+            @pl.when(p >= LAG)
+            def _():
+                last(p - LAG)
+
+            for q in range(nq):
+                @pl.when(p == LAG + (q + 1) * (pieces // nq) - 1)
+                def _():
+                    share(q)
+
+        loop(pieces + LAG, turn)
 
     for q in range(nq):
         total = quarter(q, aux, orb)
@@ -393,6 +413,7 @@
         occ = amplitudes.shape[-1]
         line = mesh.shape["ka"] == 4 and mesh.shape["aux"] == 2 and mesh.shape["orb"] == 2
         fits = rows % math.lcm(occ, LANES) == 0 and vdev % (BUNCH * ROWS_EACH) == 0 and occ % 32 == 0
+        fits = fits and nq * rows * vdev >= AHEAD * math.lcm(occ, LANES) * ROWS_EACH
         chosen = line_body if line and fits else ring_body
         return chosen(chol_tiles, tile_exps, amplitudes, pair_table)
 

time: 42.6 us -> 42.6 us (level)
  no operation moved by 1% of the time
where the time goes in v4:
time: 42.6 us; the launch traced here: 42.4 us
  Pallas kernels  41.8 us (98%)
  between operations  0.64 us (2%)
    pallas_call x1, Pallas kernels, line_body(): pl.pallas_call(functools.partial(line_kernel, (nq, occ, vdev, width, grou...  39.9 us
    pallas_call x1, Pallas kernels, line_body(): pl.pallas_call(hand_on, out_shape=(jax.ShapeDtypeStruct(dressed.shape, dr...  1.89 us

profile of v4, /device:TPU:0, one launch (start us, length us, event | category | flops | bytes accessed | tf_op | source)
XLA Modules:
  0.0 42.4 jit_solution(9545655177272400859)
XLA Ops:
  0.6 39.9 %shard_map.59 = (bf16[2,1,192,768]{3,2,1,0:T(8,128)(2,1)}, f32[2,1,24,96]{3,2,1,0:T(8,128)}) custom-call(bf16[2,1,192,768]{3,2,1,0:T(8,128)(2,1)} %bitcast.2, bf16[2,1,4,96,96]{4,3,2,1,0:T(8,128)(2,1)} %amps_far.1, s32[2,1,6]{2,1,0:T(1,128)} %exps_far.1, s32[4,4]{1,0:T(4,128)} %table_far.1), custom_call_target="tpu_custom_call" | custom-call | flops 452984832 | bytes 1179648 | tf_op jit(solution)/shard_map/pallas_call | solution.py:327
  40.5 1.9 %hand_on.1 = (bf16[2,1,192,768]{3,2,1,0:T(8,128)(2,1)}, f32[2,1,24,96]{3,2,1,0:T(8,128)}) custom-call(bf16[2,1,192,768]{3,2,1,0:T(8,128)(2,1)} %get-tuple-element.6.near_out, f32[2,1,24,96]{3,2,1,0:T(8,128)} %get-tuple-element.7.near_cycle), custom_call_target="tpu_custom_call" | custom-call | tf_op jit(solution)/shard_map/hand_on/pallas_call | solution.py:391
